TPU v7x, 32 devices: a whole 2x2x4 slice. The times are simulated.
32 devices in a mesh: wide: 8 (over z, x), narrow: 4 (over y, core).
Axes of the slice: x: 2, y: 2, z: 4, core: 2. Of those that a mesh axis runs over, the one named last changes fastest.
Arguments:
- fields: bfloat16 [24, 128, 8, 512], P(None, None, 'wide', 'narrow'), may hold values from -6 to 6
- neighbors: int32 [4, 8, 512], P(None, 'wide', 'narrow'), may hold values from 0 to 511, as said below
- cost: int32 [8, 512], P('wide', 'narrow'), may hold values from 1 to 8
- dest: int32 [8, 512], P('wide', 'narrow'), may hold values from 0 to 31, as said below
- diffusivity: bfloat16 [128, 8, 512], P(None, 'wide', 'narrow'), may hold values from 0.099609375 to 1
- operators: bfloat16 [8, 128, 128], replicated
Outputs:
- new_fields: bfloat16 [24, 128, 8, 512], P(None, None, 'wide', 'narrow')
- column_burden: float32 [32, 24, 128], P(('wide', 'narrow'))
Inputs may be any that keep to these rules, and one draw needn't show every extreme that they name: neighbors[k, r, c] lies within 2 columns of c along the row, counted cyclically over 512, and is never c. `dest`: stretch w * (narrow devices) + n is the device at index w of wide and n of narrow. Of the columns of one device, at most 8 go to one stretch, and exactly 8 go to some stretches; every stretch receives exactly 128 columns in all. Each device deals its columns, in order of rising cost, to its stretches in turn, so that the stretches' summed costs are nearly even while the grid blocks' are not.
All inputs are finite; a program needn't handle non-finite values.
Results may differ from a plain program's by a relative error of at most 0.0068.
Values may be sent and summed in bfloat16 or wider, within the bound.
A program may use at most 64 MiB of HBM per device.

v0:
```python
import functools

import jax
import jax.numpy as jnp
from jax import lax
from jax.experimental import pallas as pl
from jax.experimental.pallas import tpu as pltpu
from jax.sharding import PartitionSpec as P

REACH = 2
EDGES = 2 * REACH
MESH = pl.DeviceIdType.MESH
F32 = jnp.float32
BF16 = jnp.bfloat16
I32 = jnp.int32


def iota(shape, dim):
    return lax.broadcasted_iota(I32, shape, dim)


def ones_at(mask):
    return jnp.where(mask, 1.0, 0.0).astype(F32)


def dot(a, b):
    return jnp.dot(a, b, preferred_element_type=F32)


def dot_nt(a, b):
    return lax.dot_general(a, b, (((1,), (1,)), ((), ())), preferred_element_type=F32)


def dot_tn(a, b):
    return lax.dot_general(a, b, (((0,), (0,)), ((), ())), preferred_element_type=F32)


def three_parts(values):
    high = values.astype(BF16)
    rest = values - high.astype(F32)
    mid = rest.astype(BF16)
    low = (rest - mid.astype(F32)).astype(BF16)
    return high, mid, low


def kernel(
    wide_n, narrow_n, slots,
    x_ref, nb_ref, cost_ref, dest_ref, diff_ref, op_ref,
    new_ref, burden_ref,
    both_ref, dyn_ref, cur_ref, ge_ref, pack_ref, halo_ref, sums_ref, out_slots, in_slots,
    halo_send, halo_recv, slot_send, slot_recv,
):
    tracer_n, level_n, col_n = x_ref.shape
    substep_n = op_ref.shape[0]
    dev_n = wide_n * narrow_n
    row_span = narrow_n * col_n
    wide = lax.axis_index("wide")
    narrow = lax.axis_index("narrow")
    me = wide * narrow_n + narrow
    base = narrow * col_n

    barrier = pltpu.get_barrier_semaphore()

    def greet(i, carry):
        other = lax.rem(me + i, dev_n)
        pl.semaphore_signal(
            barrier, inc=1, device_id=(other // narrow_n, lax.rem(other, narrow_n)), device_id_type=MESH
        )
        return carry

    lax.fori_loop(1, dev_n, greet, 0)

    src = iota((col_n, col_n), 0)
    lane = iota((col_n, col_n), 1)
    k = lane & (EDGES - 1)
    edge_col = jnp.where(k < REACH, k, col_n - EDGES + k)
    pick = src == edge_col
    group = lax.shift_right_logical(lane, 2)
    packed = jnp.zeros((level_n, col_n), F32)
    for q in range(tracer_n):
        packed += dot(x_ref[q], ones_at(pick & (group == q)).astype(BF16))
    pack_ref[...] = packed.astype(BF16)

    pl.semaphore_wait(barrier, dev_n - 1)
    copies = []
    for side, step in ((0, 1), (1, narrow_n - 1)):
        copies.append(
            pltpu.make_async_remote_copy(
                src_ref=pack_ref,
                dst_ref=halo_ref.at[side],
                send_sem=halo_send.at[side],
                recv_sem=halo_recv.at[side],
                device_id=(wide, lax.rem(narrow + step, narrow_n)),
                device_id_type=MESH,
            )
        )
    for copy in copies:
        copy.start()

    rows = iota((level_n, level_n), 0)
    cols = iota((level_n, level_n), 1)
    second = (
        ones_at(cols == jnp.maximum(rows - 1, 0))
        + ones_at(cols == jnp.minimum(rows + 1, level_n - 1))
        - 2.0 * ones_at(cols == rows)
    ).astype(BF16)
    for s in range(substep_n):
        both_ref[s, :level_n, :] = op_ref[s]
        both_ref[s, level_n:, :] = dot(second, op_ref[s]).astype(BF16)
    cost = cost_ref[...]
    ge = diff_ref[...].astype(F32) * (cost.astype(F32) / (4.0 * substep_n))
    ge_ref[:, :col_n] = ge
    ge_ref[:, col_n:] = ge

    near = ones_at(src == lane)
    side_row = iota((col_n, col_n), 0) & (EDGES - 1)
    left_of = jnp.where(
        side_row >= REACH, lax.rem(base + row_span - EDGES + side_row, row_span), -1
    )
    right_of = jnp.where(side_row < REACH, lax.rem(base + col_n + side_row, row_span), -1)
    from_left = jnp.zeros((col_n, col_n), F32)
    from_right = jnp.zeros((col_n, col_n), F32)
    for n in range(nb_ref.shape[0]):
        neighbor = nb_ref[n : n + 1, :]
        near += ones_at(src == neighbor - base)
        from_left += ones_at(left_of == neighbor)
        from_right += ones_at(right_of == neighbor)
    near = near.astype(BF16)
    row_group = lax.shift_right_logical(src, 2)

    for copy in copies:
        copy.wait()
    left = halo_ref[0]
    right = halo_ref[1]
    for q in range(tracer_n):
        mine = row_group == q
        total = (
            dot(x_ref[q], near)
            + dot(left, jnp.where(mine, from_left, 0.0).astype(BF16))
            + dot(right, jnp.where(mine, from_right, 0.0).astype(BF16))
        )
        dyn = (0.2 * total).astype(BF16)
        dyn_ref[q] = dyn
        cur_ref[q // 2, :, (q % 2) * col_n : (q % 2 + 1) * col_n] = dyn.astype(F32)

    cost_two = jnp.concatenate([cost, cost], axis=1)

    def substep(s, carry):
        both = both_ref[s]
        live = cost_two > s
        for p in range(cur_ref.shape[0]):
            now = cur_ref[p]
            mixed = dot(both, now.astype(BF16))
            moved = mixed[:level_n] + ge_ref[...] * mixed[level_n:]
            cur_ref[p] = jnp.where(live, moved, now)
        return carry

    lax.fori_loop(0, substep_n, substep, 0)

    sums_ref[...] = jnp.ones(sums_ref.shape, F32)
    for q in range(tracer_n):
        change = cur_ref[q // 2, :, (q % 2) * col_n : (q % 2 + 1) * col_n] - dyn_ref[q].astype(F32)
        sums_ref[q : q + 1, :] = jnp.sum(change, axis=0, keepdims=True)
    dest = dest_ref[...]
    hot = ones_at(iota((dev_n, col_n), 0) == dest)
    earlier = dot(hot.astype(BF16), ones_at(src < lane).astype(BF16))
    placed = jnp.sum(hot * earlier, axis=0, keepdims=True).astype(I32)
    spot = ones_at(iota((dev_n * slots, col_n), 0) == dest * slots + placed).astype(BF16)
    filled = jnp.zeros((dev_n * slots, col_n), F32)
    for part in three_parts(sums_ref[...]):
        filled += dot_nt(spot, part)
    filled = filled.reshape(dev_n, slots, col_n)
    out_slots[...] = filled
    in_slots[me] = out_slots[me]

    def send(i, carry):
        other = lax.rem(me + i, dev_n)
        pltpu.make_async_remote_copy(
            src_ref=out_slots.at[other],
            dst_ref=in_slots.at[me],
            send_sem=slot_send,
            recv_sem=slot_recv,
            device_id=(other // narrow_n, lax.rem(other, narrow_n)),
            device_id_type=MESH,
        ).start()
        return carry

    lax.fori_loop(1, dev_n, send, 0)

    for q in range(tracer_n):
        dyn = dyn_ref[q].astype(F32)
        change = cur_ref[q // 2, :, (q % 2) * col_n : (q % 2 + 1) * col_n] - dyn
        new_ref[q] = (dyn + change.astype(BF16).astype(F32)).astype(BF16)

    slot_n = dev_n * slots
    before = ones_at(iota((slot_n, slot_n), 1) < iota((slot_n, slot_n), 0)).astype(BF16)

    others = pl.ds(0, dev_n - 1)
    pltpu.make_async_copy(in_slots.at[others], in_slots.at[others], slot_recv).wait()
    pltpu.make_async_copy(out_slots.at[others], out_slots.at[others], slot_send).wait()
    got = in_slots[...].reshape(slot_n, col_n)
    valid = jnp.broadcast_to(got[:, col_n - 1 :], (slot_n, col_n))
    rank = dot(before, valid.astype(BF16))
    chosen = jnp.where(rank == iota((slot_n, col_n), 1).astype(F32), valid, 0.0).astype(BF16)
    total = jnp.zeros((col_n, col_n), F32)
    for part in three_parts(got):
        total += dot_tn(part, chosen)
    burden_ref[...] = total[:tracer_n]


def local(mesh_shape, fields, neighbors, cost, dest, diffusivity, operators):
    tracer_n, level_n, row_n, col_n = fields.shape
    substep_n = operators.shape[0]
    wide_n, narrow_n = mesh_shape
    dev_n = wide_n * narrow_n
    assert row_n == 1 and tracer_n % 2 == 0 and tracer_n * EDGES <= col_n
    slots = -(-(2 * col_n // dev_n) // 8) * 8
    vmem = pl.BlockSpec(memory_space=pltpu.VMEM)
    new, burden = pl.pallas_call(
        functools.partial(kernel, wide_n, narrow_n, slots),
        out_shape=(
            jax.ShapeDtypeStruct((tracer_n, level_n, col_n), BF16),
            jax.ShapeDtypeStruct((tracer_n, col_n), F32),
        ),
        in_specs=[vmem] * 6,
        out_specs=(vmem, vmem),
        scratch_shapes=[
            pltpu.VMEM((substep_n, 2 * level_n, level_n), BF16),
            pltpu.VMEM((tracer_n, level_n, col_n), BF16),
            pltpu.VMEM((tracer_n // 2, level_n, 2 * col_n), F32),
            pltpu.VMEM((level_n, 2 * col_n), F32),
            pltpu.VMEM((level_n, col_n), BF16),
            pltpu.VMEM((2, level_n, col_n), BF16),
            pltpu.VMEM((col_n, col_n), F32),
            pltpu.VMEM((dev_n, slots, col_n), F32),
            pltpu.VMEM((dev_n, slots, col_n), F32),
            pltpu.SemaphoreType.DMA((2,)),
            pltpu.SemaphoreType.DMA((2,)),
            pltpu.SemaphoreType.DMA,
            pltpu.SemaphoreType.DMA,
        ],
        compiler_params=pltpu.CompilerParams(
            collective_id=0, has_side_effects=True, vmem_limit_bytes=40 * 1024 * 1024
        ),
    )(
        fields.reshape(tracer_n, level_n, col_n),
        neighbors.reshape(neighbors.shape[0], col_n),
        cost,
        dest,
        diffusivity.reshape(level_n, col_n),
        operators,
    )
    return new.reshape(fields.shape), burden[None]


def solution(mesh):
    in_specs = (
        P(None, None, "wide", "narrow"),
        P(None, "wide", "narrow"),
        P("wide", "narrow"),
        P("wide", "narrow"),
        P(None, "wide", "narrow"),
        P(),
    )
    out_specs = (P(None, None, "wide", "narrow"), P(("wide", "narrow"), None, None))
    mesh_shape = (mesh.shape["wide"], mesh.shape["narrow"])
    return jax.shard_map(
        functools.partial(local, mesh_shape),
        mesh=mesh,
        in_specs=in_specs,
        out_specs=out_specs,
        check_vma=False,
    )
```

profile of v0, /device:TPU:0, one launch (start us, length us, event | category | flops | bytes accessed | tf_op | source)
XLA Modules:
  0.0 25.3 jit_solution(4554466176788516263)
XLA Ops:
  0.6 0.0 copy-start.3
  0.6 0.0 copy-start.4
  0.7 0.0 copy-start.5
  0.7 0.7 %copy-done.3 = s32[4,1,128]{2,1,0:T(1,128)S(1)} copy-done((s32[4,1,128]{2,1,0:T(1,128)S(1)}, s32[4,1,128]{2,1,0:T(1,128)}, u32[]{:S(2)}) %copy-start.3) | copy-done | bytes 2072
  1.3 0.0 copy-done.4
  1.3 0.0 copy-done.5
  1.3 0.0 copy-start
  1.3 1.1 %copy-done = bf16[24,128,1,128]{3,1,2,0:T(8,128)(2,1)S(1)} copy-done((bf16[24,128,1,128]{3,1,2,0:T(8,128)(2,1)S(1)}, bf16[24,128,1,128]{3,1,2,0:T(8,128)(2,1)}, u32[]{:S(2)}) %copy-start) | copy-done | bytes 786456
  2.5 0.0 copy-start.1
  2.5 0.9 %copy-done.1 = bf16[8,128,128]{2,1,0:T(8,128)(2,1)S(1)} copy-done((bf16[8,128,128]{2,1,0:T(8,128)(2,1)S(1)}, bf16[8,128,128]{2,1,0:T(8,128)(2,1)}, u32[]{:S(2)}) %copy-start.1) | copy-done | bytes 262168
  3.4 0.0 copy-start.2
  3.4 0.8 %copy-done.2 = bf16[128,1,128]{2,0,1:T(8,128)(2,1)S(1)} copy-done((bf16[128,1,128]{2,0,1:T(8,128)(2,1)S(1)}, bf16[128,1,128]{2,0,1:T(8,128)(2,1)}, u32[]{:S(2)}) %copy-start.2) | copy-done | bytes 32792
  4.2 19.6 %shard_map.77 = (bf16[24,128,128]{2,1,0:T(8,128)(2,1)S(1)}, f32[24,128]{1,0:T(8,128)S(1)}) custom-call(bf16[24,128,128]{2,1,0:T(8,128)(2,1)S(1)} %bitcast.7, s32[4,128]{1,0:T(4,128)S(1)} %bitcast.11, s32[1,128]{1,0:T(1,128)S(1)} %copy-done.4, s32[1,128]{1,0:T(1,128)S(1)} %copy-done.5, bf16[128,128]{1,0:T(8,128)(2,1)S(1)} %bitcast.9, ...), custom_call_target="tpu_custom_call" | custom-call | tf_op jit(solution)/shard_map/pallas_call | solution.py:219
  23.8 0.9 %copy.11 = bf16[24,128,1,128]{3,1,2,0:T(8,128)(2,1)} copy(bf16[24,128,1,128]{3,1,2,0:T(8,128)(2,1)S(1)} %bitcast.8) | data formatting | bytes 1572864
  24.7 0.6 %copy.12 = f32[1,24,128]{2,1,0:T(8,128)} copy(f32[1,24,128]{2,1,0:T(8,128)S(1)} %bitcast.10) | data formatting | bytes 24576
Async XLA Ops:
  0.6 0.7 %copy-start.3 = (s32[4,1,128]{2,1,0:T(1,128)S(1)}, s32[4,1,128]{2,1,0:T(1,128)}, u32[]{:S(2)}) copy-start(s32[4,1,128]{2,1,0:T(1,128)} %param.7) | copy-start | bytes 6148
  0.6 0.7 %copy-start.4 = (s32[1,128]{1,0:T(1,128)S(1)}, s32[1,128]{1,0:T(1,128)}, u32[]{:S(2)}) copy-start(s32[1,128]{1,0:T(1,128)} %cost_ref.1) | copy-start | bytes 1540
  0.7 0.7 %copy-start.5 = (s32[1,128]{1,0:T(1,128)S(1)}, s32[1,128]{1,0:T(1,128)}, u32[]{:S(2)}) copy-start(s32[1,128]{1,0:T(1,128)} %dest_ref.1) | copy-start | bytes 1540
  1.3 1.1 %copy-start = (bf16[24,128,1,128]{3,1,2,0:T(8,128)(2,1)S(1)}, bf16[24,128,1,128]{3,1,2,0:T(8,128)(2,1)}, u32[]{:S(2)}) copy-start(bf16[24,128,1,128]{3,1,2,0:T(8,128)(2,1)} %param.6) | copy-start | bytes 2359300
  2.5 0.9 %copy-start.1 = (bf16[8,128,128]{2,1,0:T(8,128)(2,1)S(1)}, bf16[8,128,128]{2,1,0:T(8,128)(2,1)}, u32[]{:S(2)}) copy-start(bf16[8,128,128]{2,1,0:T(8,128)(2,1)} %op_ref.1) | copy-start | bytes 786436
  3.4 0.8 %copy-start.2 = (bf16[128,1,128]{2,0,1:T(8,128)(2,1)S(1)}, bf16[128,1,128]{2,0,1:T(8,128)(2,1)}, u32[]{:S(2)}) copy-start(bf16[128,1,128]{2,0,1:T(8,128)(2,1)} %param.10) | copy-start | bytes 98308
where the time goes:
time: 25.5 us; the launch traced here: 25.3 us
  Pallas kernels  19.6 us (77%)
  local copies, waits for them, and re-layouts  4.98 us (20%)
  between operations  0.67 us (3%)
    pallas_call x1, Pallas kernels, local(): pl.pallas_call(functools.partial(kernel, wide_n, narrow_n, slots), out_sh...  19.6 us
    unnamed x14, local copies, waits for them, and re-layouts  4.98 us

commit v1 on v0

v1 whole, which is shorter than its diff:
```python
import functools

import jax
import jax.numpy as jnp
from jax import lax
from jax.experimental import pallas as pl
from jax.experimental.pallas import tpu as pltpu
from jax.sharding import PartitionSpec as P

REACH = 2
EDGES = 2 * REACH
MESH = pl.DeviceIdType.MESH
F32 = jnp.float32
BF16 = jnp.bfloat16
I32 = jnp.int32


def iota(shape, dim):
    return lax.broadcasted_iota(I32, shape, dim)


def ones_at(mask):
    return jnp.where(mask, 1.0, 0.0).astype(F32)


def dot(a, b):
    return jnp.dot(a, b, preferred_element_type=F32)


def dot_nt(a, b):
    return lax.dot_general(a, b, (((1,), (1,)), ((), ())), preferred_element_type=F32)


def dot_tn(a, b):
    return lax.dot_general(a, b, (((0,), (0,)), ((), ())), preferred_element_type=F32)


def wrap(index, size):
    return jnp.where(index >= size, index - size, index)


def kernel(
    wide_n, narrow_n, slots, group_n,
    x_hbm, nb_hbm, cost_hbm, dest_hbm, diff_hbm, op_hbm,
    new_ref, got_ref,
    x_ref, nb_ref, cost_ref, dest_ref, diff_ref, op_ref,
    both_ref, dyn_ref, cur_ref, ge_ref, pack_ref, halo_ref,
    edge_ge, edge_sum, edge_dyn, edge_cur, spot_ref, sums_ref, out_slots, in_slots,
    in_sem, x_sem, halo_send, halo_recv, slot_send, slot_recv,
):
    tracer_n, level_n, col_n = x_ref.shape
    substep_n = op_ref.shape[0]
    dev_n = wide_n * narrow_n
    row_span = narrow_n * col_n
    pair_n = tracer_n // 2
    chunk_n = x_sem.shape[0]
    chunk = tracer_n // chunk_n
    wide = lax.axis_index("wide")
    narrow = lax.axis_index("narrow")
    me = wide * narrow_n + narrow
    base = narrow * col_n

    loads = []
    for index, (far, here) in enumerate(
        ((nb_hbm, nb_ref), (cost_hbm, cost_ref), (dest_hbm, dest_ref), (diff_hbm, diff_ref), (op_hbm, op_ref))
    ):
        loads.append(pltpu.make_async_copy(far, here, in_sem.at[index]))
    x_loads = []
    for index in range(chunk_n):
        part = pl.ds(index * chunk, chunk)
        x_loads.append(pltpu.make_async_copy(x_hbm.at[part], x_ref.at[part], x_sem.at[index]))
    for load in loads[:1] + x_loads + loads[1:]:
        load.start()

    partners = []
    for dw in range(wide_n):
        for dn in range(narrow_n):
            if dw or dn:
                partners.append((wrap(wide + dw, wide_n), wrap(narrow + dn, narrow_n)))
    barrier = pltpu.get_barrier_semaphore()
    for partner in partners:
        pl.semaphore_signal(barrier, inc=1, device_id=partner, device_id_type=MESH)

    src = iota((col_n, col_n), 0)
    lane = iota((col_n, col_n), 1)
    lane_k = lane & (EDGES - 1)
    row_k = src & (EDGES - 1)
    edge_col = jnp.where(lane_k < REACH, col_n - REACH + lane_k, lane_k - REACH)
    pick = ones_at(src == edge_col).astype(BF16)
    shift = EDGES.bit_length() - 1
    lane_q = lax.shift_right_logical(lane, shift)
    row_q = lax.shift_right_logical(src, shift)
    same_q = row_q == lane_q
    left_of = jnp.where(row_k < REACH, lax.rem(base + row_span - REACH + row_k, row_span), -1)
    right_of = jnp.where(row_k >= REACH, lax.rem(base + col_n + row_k - REACH, row_span), -1)

    loads[0].wait()
    near = ones_at(src == lane)
    from_left = jnp.zeros((col_n, col_n), F32)
    from_right = jnp.zeros((col_n, col_n), F32)
    for n in range(nb_ref.shape[0]):
        neighbor = nb_ref[n : n + 1, :]
        near += ones_at(src == neighbor - base)
        from_left += ones_at(left_of == neighbor)
        from_right += ones_at(right_of == neighbor)
    near = near.astype(BF16)

    def edge_shift(q):
        return (EDGES * q + REACH) % col_n

    packed = jnp.zeros((level_n, col_n), F32)
    partial = jnp.zeros((level_n, col_n), F32)
    for q in range(tracer_n):
        if q % chunk == 0:
            x_loads[q // chunk].wait()
        x = x_ref[q]
        total = dot(x, near)
        packed = jnp.where(lane_q == q, pltpu.roll(x.astype(F32), edge_shift(q), 1), packed)
        partial = jnp.where(lane_q == q, pltpu.roll(total, edge_shift(q), 1), partial)
        dyn = (0.2 * total).astype(BF16)
        dyn_ref[q] = dyn
        cur_ref[q // 2, :, (q % 2) * col_n : (q % 2 + 1) * col_n] = dyn.astype(F32)
    pack_ref[...] = packed.astype(BF16)

    pl.semaphore_wait(barrier, dev_n - 1)
    copies = []
    for side, step in ((0, 1), (1, narrow_n - 1)):
        copies.append(
            pltpu.make_async_remote_copy(
                src_ref=pack_ref,
                dst_ref=halo_ref.at[side],
                send_sem=halo_send.at[side],
                recv_sem=halo_recv.at[side],
                device_id=(wide, wrap(narrow + step, narrow_n)),
                device_id_type=MESH,
            )
        )
    for copy in copies:
        copy.start()

    for load in loads[1:]:
        load.wait()
    rows = iota((level_n, level_n), 0)
    cols = iota((level_n, level_n), 1)
    second = (
        ones_at(cols == jnp.maximum(rows - 1, 0))
        + ones_at(cols == jnp.minimum(rows + 1, level_n - 1))
        - 2.0 * ones_at(cols == rows)
    ).astype(BF16)
    for s in range(substep_n):
        both_ref[s, :level_n, :] = op_ref[s]
        both_ref[s, level_n:, :] = dot(second, op_ref[s]).astype(BF16)
    cost = cost_ref[...]
    gain = cost.astype(F32) / (4.0 * substep_n)
    ge = diff_ref[...].astype(F32) * gain
    ge_ref[:, :col_n] = ge
    ge_ref[:, col_n:] = ge

    edge_cost = dot(jnp.broadcast_to(cost.astype(F32), (16, col_n)).astype(BF16), pick)[:1]
    edge_ge[...] = dot(diff_ref[...], pick) * (edge_cost / (4.0 * substep_n))
    edge_sum[...] = partial
    edge_left = jnp.where(same_q, dot(from_left.astype(BF16), pick), 0.0).astype(BF16)
    edge_right = jnp.where(same_q, dot(from_right.astype(BF16), pick), 0.0).astype(BF16)

    dest = dest_ref[...]
    hot = ones_at(iota((dev_n, col_n), 0) == dest)
    earlier = dot(hot.astype(BF16), ones_at(src < lane).astype(BF16))
    placed = jnp.sum(hot * earlier, axis=0, keepdims=True).astype(I32)
    spot_ref[...] = ones_at(iota((slots * dev_n, col_n), 0) == placed * dev_n + dest).astype(BF16)

    cost_two = jnp.concatenate([cost, cost], axis=1)

    def advance(s, pairs):
        both = both_ref[s]
        live = cost_two > s
        for p in pairs:
            now = cur_ref[p]
            mixed = dot(both, now.astype(BF16))
            moved = mixed[:level_n] + ge_ref[...] * mixed[level_n:]
            cur_ref[p] = jnp.where(live, moved, now)

    def leading_half(s, carry):
        advance(s, range(pair_n // 2))
        return carry

    lax.fori_loop(0, substep_n, leading_half, 0, unroll=2)

    for copy in copies:
        copy.wait()
    total = edge_sum[...] + dot(halo_ref[0], edge_left) + dot(halo_ref[1], edge_right)
    start = (0.2 * total).astype(BF16)
    edge_dyn[...] = start
    edge_cur[...] = start.astype(F32)

    def other_half(s, carry):
        advance(s, range(pair_n // 2, pair_n))
        now = edge_cur[...]
        mixed = dot(both_ref[s], now.astype(BF16))
        moved = mixed[:level_n] + edge_ge[...] * mixed[level_n:]
        edge_cur[...] = jnp.where(edge_cost > s.astype(F32), moved, now)
        return carry

    lax.fori_loop(0, substep_n, other_half, 0, unroll=2)

    edge_start = edge_dyn[...].astype(F32)
    edge_change = edge_cur[...] - edge_start
    edge_burden = jnp.broadcast_to(jnp.sum(edge_change, axis=0, keepdims=True), (8, col_n))
    col = iota((1, col_n), 1)
    inner = (col >= REACH) & (col < col_n - REACH)
    sums_ref[...] = jnp.ones(sums_ref.shape, F32)
    for q in range(tracer_n):
        change = cur_ref[q // 2, :, (q % 2) * col_n : (q % 2 + 1) * col_n] - dyn_ref[q].astype(F32)
        outer = pltpu.roll(edge_burden, col_n - edge_shift(q), 1)[:1]
        sums_ref[q : q + 1, :] = jnp.where(inner, jnp.sum(change, axis=0, keepdims=True), outer)
    per_row = col_n // group_n
    sums = sums_ref[...]
    sums = jnp.concatenate([sums] * per_row, axis=0)
    high = sums.astype(BF16)
    low = (sums - high.astype(F32)).astype(BF16)
    filled = dot_nt(spot_ref[...], high) + dot_nt(spot_ref[...], low)
    lane_group = iota((dev_n, col_n), 1) // group_n
    lines = []
    for begin in range(0, slots, per_row):
        line = jnp.zeros((dev_n, col_n), F32)
        for m in range(min(per_row, slots - begin)):
            line = jnp.where(lane_group == m, filled[(begin + m) * dev_n : (begin + m + 1) * dev_n], line)
        lines.append(line)
    line = jnp.concatenate(lines, axis=1)
    for h in range(dev_n):
        out_slots[h] = line[h : h + 1]
    in_slots[me] = out_slots[me]
    for far_wide, far_narrow in partners:
        pltpu.make_async_remote_copy(
            src_ref=out_slots.at[far_wide * narrow_n + far_narrow],
            dst_ref=in_slots.at[me],
            send_sem=slot_send,
            recv_sem=slot_recv,
            device_id=(far_wide, far_narrow),
            device_id_type=MESH,
        ).start()

    edge_new = edge_start + edge_change.astype(BF16).astype(F32)
    for q in range(tracer_n):
        dyn = dyn_ref[q].astype(F32)
        change = cur_ref[q // 2, :, (q % 2) * col_n : (q % 2 + 1) * col_n] - dyn
        new = dyn + change.astype(BF16).astype(F32)
        outer = pltpu.roll(edge_new, col_n - edge_shift(q), 1)
        new_ref[q] = jnp.where(inner, new, outer).astype(BF16)

    others = pl.ds(0, dev_n - 1)
    pltpu.make_async_copy(in_slots.at[others], in_slots.at[others], slot_recv).wait()
    pltpu.make_async_copy(out_slots.at[others], out_slots.at[others], slot_send).wait()
    for h in range(dev_n):
        got_ref[h : h + 1, :] = in_slots[h]


def finish(slots, group_n, tracer_n, new_ref, got_ref, new_hbm, burden_hbm, burden_ref, sem):
    dev_n = got_ref.shape[0]
    col_n = burden_ref.shape[1]
    copy = pltpu.make_async_copy(new_ref, new_hbm, sem.at[0])
    copy.start()
    got = got_ref[...]
    width = got.shape[1]
    per_row = col_n // group_n
    flag = jnp.where(lax.rem(iota(got.shape, 1), group_n) == tracer_n, got, 0.0).astype(BF16)
    count = dot(flag, jnp.ones((width, col_n), BF16))
    before = ones_at(iota((dev_n, dev_n), 1) < iota((dev_n, dev_n), 0)).astype(BF16)
    rank = iota((dev_n, col_n), 1).astype(F32) - dot(before, count.astype(BF16))
    high = got.astype(BF16)
    low = (got - high.astype(F32)).astype(BF16)
    total = jnp.zeros((tracer_n, col_n), F32)
    for row, begin in enumerate(range(0, slots, per_row)):
        members = range(begin, min(begin + per_row, slots))
        chosen = jnp.concatenate(
            [ones_at((rank == float(k)) & (count > float(k))).astype(BF16) for k in members], axis=1
        )
        span = slice(row * col_n, (row + 1) * col_n)
        placed = dot_tn(high[:, span], chosen) + dot_tn(low[:, span], chosen)
        for m in range(len(members)):
            total += placed[m * group_n : m * group_n + tracer_n, m * col_n : (m + 1) * col_n]
    burden_ref[...] = total
    second = pltpu.make_async_copy(burden_ref, burden_hbm, sem.at[1])
    second.start()
    second.wait()
    copy.wait()


def local(mesh_shape, fields, neighbors, cost, dest, diffusivity, operators):
    tracer_n, level_n, row_n, col_n = fields.shape
    substep_n = operators.shape[0]
    neighbor_n = neighbors.shape[0]
    wide_n, narrow_n = mesh_shape
    dev_n = wide_n * narrow_n
    group_n = 1 << tracer_n.bit_length()
    slots = 2 * col_n // dev_n
    assert row_n == 1 and tracer_n % 4 == 0 and tracer_n * EDGES <= col_n and group_n <= col_n
    width = -(-slots * group_n // col_n) * col_n
    hbm = pl.BlockSpec(memory_space=pltpu.HBM)
    vmem = pl.BlockSpec(memory_space=pltpu.VMEM)
    chunk_n = 4
    operands = (
        fields.reshape(tracer_n, level_n, col_n),
        neighbors.reshape(neighbor_n, col_n),
        cost,
        dest,
        diffusivity.reshape(level_n, col_n),
        operators,
    )
    new, got = pl.pallas_call(
        functools.partial(kernel, wide_n, narrow_n, slots, group_n),
        out_shape=(
            jax.ShapeDtypeStruct((tracer_n, level_n, col_n), BF16),
            jax.ShapeDtypeStruct((dev_n, width), F32),
        ),
        in_specs=[hbm] * 6,
        out_specs=(vmem, vmem),
        scratch_shapes=[
            pltpu.VMEM((tracer_n, level_n, col_n), BF16),
            pltpu.VMEM((neighbor_n, col_n), I32),
            pltpu.VMEM((1, col_n), I32),
            pltpu.VMEM((1, col_n), I32),
            pltpu.VMEM((level_n, col_n), BF16),
            pltpu.VMEM((substep_n, level_n, level_n), BF16),
            pltpu.VMEM((substep_n, 2 * level_n, level_n), BF16),
            pltpu.VMEM((tracer_n, level_n, col_n), BF16),
            pltpu.VMEM((tracer_n // 2, level_n, 2 * col_n), F32),
            pltpu.VMEM((level_n, 2 * col_n), F32),
            pltpu.VMEM((level_n, col_n), BF16),
            pltpu.VMEM((2, level_n, col_n), BF16),
            pltpu.VMEM((level_n, col_n), F32),
            pltpu.VMEM((level_n, col_n), F32),
            pltpu.VMEM((level_n, col_n), BF16),
            pltpu.VMEM((level_n, col_n), F32),
            pltpu.VMEM((slots * dev_n, col_n), BF16),
            pltpu.VMEM((group_n, col_n), F32),
            pltpu.VMEM((dev_n, 1, width), F32),
            pltpu.VMEM((dev_n, 1, width), F32),
            pltpu.SemaphoreType.DMA((5,)),
            pltpu.SemaphoreType.DMA((chunk_n,)),
            pltpu.SemaphoreType.DMA((2,)),
            pltpu.SemaphoreType.DMA((2,)),
            pltpu.SemaphoreType.DMA,
            pltpu.SemaphoreType.DMA,
        ],
        compiler_params=pltpu.CompilerParams(
            collective_id=0, has_side_effects=True, vmem_limit_bytes=40 * 1024 * 1024
        ),
    )(*[pltpu.with_memory_space_constraint(value, pltpu.HBM) for value in operands])
    new, burden = pl.pallas_call(
        functools.partial(finish, slots, group_n, tracer_n),
        out_shape=(
            jax.ShapeDtypeStruct((tracer_n, level_n, col_n), BF16),
            jax.ShapeDtypeStruct((tracer_n, col_n), F32),
        ),
        in_specs=[vmem, vmem],
        out_specs=(hbm, hbm),
        scratch_shapes=[pltpu.VMEM((tracer_n, col_n), F32), pltpu.SemaphoreType.DMA((2,))],
    )(new, got)
    return new.reshape(fields.shape), burden[None]


def solution(mesh):
    in_specs = (
        P(None, None, "wide", "narrow"),
        P(None, "wide", "narrow"),
        P("wide", "narrow"),
        P("wide", "narrow"),
        P(None, "wide", "narrow"),
        P(),
    )
    out_specs = (P(None, None, "wide", "narrow"), P(("wide", "narrow"), None, None))
    mesh_shape = (mesh.shape["wide"], mesh.shape["narrow"])
    return jax.shard_map(
        functools.partial(local, mesh_shape),
        mesh=mesh,
        in_specs=in_specs,
        out_specs=out_specs,
        check_vma=False,
    )
```

time: 25.5 us -> 21 us (0.82)
  local copies, waits for them, and re-layouts: 4.98 us -> 1.48 us
  Pallas kernels: 19.6 us -> 18.7 us
    unnamed x14 -> x4, local copies, waits for them, and re-layouts: 4.98 us -> 1.48 us
    pallas_call x1 -> x2, Pallas kernels: 19.6 us -> 18.7 us  [the longest x1 16.4 us: local(): pl.pallas_call(functools.partial(kernel, wide_n, narrow_n, slots, group_n...]
where the time goes in v1:
time: 21 us; the launch traced here: 20.8 us
  Pallas kernels  18.7 us (89%)
  local copies, waits for them, and re-layouts  1.48 us (7%)
  between operations  0.65 us (3%)
    pallas_call x1, Pallas kernels, local(): pl.pallas_call(functools.partial(kernel, wide_n, narrow_n, slots, group_n...  16.4 us
    pallas_call x1, Pallas kernels, local(): pl.pallas_call(functools.partial(finish, slots, group_n, tracer_n), out_s...  2.27 us
    unnamed x4, local copies, waits for them, and re-layouts  1.48 us

profile of v1, /device:TPU:0, one launch (start us, length us, event | category | flops | bytes accessed | tf_op | source)
XLA Modules:
  0.0 20.8 jit_solution(14179468207242596611)
XLA Ops:
  0.6 16.4 %shard_map.77 = (bf16[24,128,128]{2,1,0:T(8,128)(2,1)S(1)}, f32[32,256]{1,0:T(8,128)S(1)}) custom-call(bf16[24,128,128]{2,1,0:T(8,128)(2,1)} %bitcast.7, s32[4,128]{1,0:T(4,128)} %bitcast.9, s32[1,128]{1,0:T(1,128)} %cost_hbm.1, s32[1,128]{1,0:T(1,128)} %dest_hbm.1, bf16[128,128]{1,0:T(8,128)(2,1)} %bitcast.8, bf16[8,128,128]{2,1,0:T(8,128)(2,1)} %op_hbm.1), custom_call_target="tpu_custom_call" | custom-call | tf_op jit(solution)/shard_map/pallas_call | solution.py:309
  17.1 0.0 copy-start
  17.1 0.9 %copy-done = bf16[24,128,128]{2,1,0:T(8,128)(2,1)} copy-done((bf16[24,128,128]{2,1,0:T(8,128)(2,1)}, bf16[24,128,128]{2,1,0:T(8,128)(2,1)S(1)}, u32[]{:S(2)}) %copy-start) | copy-done | bytes 786456
  18.0 0.0 copy-start.1
  18.0 0.6 %copy-done.1 = f32[32,256]{1,0:T(8,128)} copy-done((f32[32,256]{1,0:T(8,128)}, f32[32,256]{1,0:T(8,128)S(1)}, u32[]{:S(2)}) %copy-start.1) | copy-done | bytes 32792
  18.6 2.3 %shard_map.78 = (bf16[24,128,128]{2,1,0:T(8,128)(2,1)}, f32[24,128]{1,0:T(8,128)}) custom-call(bf16[24,128,128]{2,1,0:T(8,128)(2,1)} %copy-done, f32[32,256]{1,0:T(8,128)} %copy-done.1), custom_call_target="tpu_custom_call" | custom-call | tf_op jit(solution)/shard_map/pallas_call | solution.py:349
Async XLA Ops:
  17.1 0.9 %copy-start = (bf16[24,128,128]{2,1,0:T(8,128)(2,1)}, bf16[24,128,128]{2,1,0:T(8,128)(2,1)S(1)}, u32[]{:S(2)}) copy-start(bf16[24,128,128]{2,1,0:T(8,128)(2,1)S(1)} %get-tuple-element.6.new_ref) | copy-start | bytes 2359300
  18.0 0.6 %copy-start.1 = (f32[32,256]{1,0:T(8,128)}, f32[32,256]{1,0:T(8,128)S(1)}, u32[]{:S(2)}) copy-start(f32[32,256]{1,0:T(8,128)S(1)} %get-tuple-element.7.got_ref) | copy-start | bytes 98308

commit v2 on v1

--- a/solution.py
+++ b/solution.py
@@ -9,6 +9,7 @@
 
 REACH = 2
 EDGES = 2 * REACH
+LAG = 2
 MESH = pl.DeviceIdType.MESH
 F32 = jnp.float32
 BF16 = jnp.bfloat16
@@ -179,11 +180,18 @@
             moved = mixed[:level_n] + ge_ref[...] * mixed[level_n:]
             cur_ref[p] = jnp.where(live, moved, now)
 
-    def leading_half(s, carry):
-        advance(s, range(pair_n // 2))
+    def advance_edge(s, now):
+        mixed = dot(both_ref[s], now.astype(BF16))
+        moved = mixed[:level_n] + edge_ge[...] * mixed[level_n:]
+        return jnp.where(edge_cost > jnp.asarray(s, F32), moved, now)
+
+    lag = min(LAG, substep_n)
+
+    def leading(s, carry):
+        advance(s, range(pair_n))
         return carry
 
-    lax.fori_loop(0, substep_n, leading_half, 0, unroll=2)
+    lax.fori_loop(0, lag, leading, 0)
 
     for copy in copies:
         copy.wait()
@@ -192,26 +200,30 @@
     edge_dyn[...] = start
     edge_cur[...] = start.astype(F32)
 
-    def other_half(s, carry):
-        advance(s, range(pair_n // 2, pair_n))
-        now = edge_cur[...]
-        mixed = dot(both_ref[s], now.astype(BF16))
-        moved = mixed[:level_n] + edge_ge[...] * mixed[level_n:]
-        edge_cur[...] = jnp.where(edge_cost > s.astype(F32), moved, now)
+    def together(s, carry):
+        advance(s, range(pair_n))
+        edge_cur[...] = advance_edge(s - lag, edge_cur[...])
         return carry
 
-    lax.fori_loop(0, substep_n, other_half, 0, unroll=2)
-
-    edge_start = edge_dyn[...].astype(F32)
-    edge_change = edge_cur[...] - edge_start
-    edge_burden = jnp.broadcast_to(jnp.sum(edge_change, axis=0, keepdims=True), (8, col_n))
+    lax.fori_loop(lag, substep_n, together, 0)
+
+    edge_end = edge_cur[...]
+    for s in range(substep_n - lag, substep_n):
+        edge_end = advance_edge(s, edge_end)
+
     col = iota((1, col_n), 1)
     inner = (col >= REACH) & (col < col_n - REACH)
+    inner_sums = []
+    for q in range(tracer_n):
+        change = cur_ref[q // 2, :, (q % 2) * col_n : (q % 2 + 1) * col_n] - dyn_ref[q].astype(F32)
+        inner_sums.append(jnp.sum(change, axis=0, keepdims=True))
+    edge_start = edge_dyn[...].astype(F32)
+    edge_change = edge_end - edge_start
+    edge_burden = jnp.broadcast_to(jnp.sum(edge_change, axis=0, keepdims=True), (8, col_n))
     sums_ref[...] = jnp.ones(sums_ref.shape, F32)
     for q in range(tracer_n):
-        change = cur_ref[q // 2, :, (q % 2) * col_n : (q % 2 + 1) * col_n] - dyn_ref[q].astype(F32)
         outer = pltpu.roll(edge_burden, col_n - edge_shift(q), 1)[:1]
-        sums_ref[q : q + 1, :] = jnp.where(inner, jnp.sum(change, axis=0, keepdims=True), outer)
+        sums_ref[q : q + 1, :] = jnp.where(inner, inner_sums[q], outer)
     per_row = col_n // group_n
     sums = sums_ref[...]
     sums = jnp.concatenate([sums] * per_row, axis=0)
@@ -257,8 +269,14 @@
 def finish(slots, group_n, tracer_n, new_ref, got_ref, new_hbm, burden_hbm, burden_ref, sem):
     dev_n = got_ref.shape[0]
     col_n = burden_ref.shape[1]
-    copy = pltpu.make_async_copy(new_ref, new_hbm, sem.at[0])
-    copy.start()
+    parts = sem.shape[0] - 1
+    size = tracer_n // parts
+    copies = []
+    for index in range(parts):
+        part = pl.ds(index * size, size)
+        copies.append(pltpu.make_async_copy(new_ref.at[part], new_hbm.at[part], sem.at[index]))
+    for copy in copies:
+        copy.start()
     got = got_ref[...]
     width = got.shape[1]
     per_row = col_n // group_n
@@ -279,10 +297,10 @@
         for m in range(len(members)):
             total += placed[m * group_n : m * group_n + tracer_n, m * col_n : (m + 1) * col_n]
     burden_ref[...] = total
-    second = pltpu.make_async_copy(burden_ref, burden_hbm, sem.at[1])
-    second.start()
-    second.wait()
-    copy.wait()
+    copies.append(pltpu.make_async_copy(burden_ref, burden_hbm, sem.at[parts]))
+    copies[-1].start()
+    for copy in copies:
+        copy.wait()
 
 
 def local(mesh_shape, fields, neighbors, cost, dest, diffusivity, operators):
@@ -354,8 +372,8 @@
         ),
         in_specs=[vmem, vmem],
         out_specs=(hbm, hbm),
-        scratch_shapes=[pltpu.VMEM((tracer_n, col_n), F32), pltpu.SemaphoreType.DMA((2,))],
-    )(new, got)
+        scratch_shapes=[pltpu.VMEM((tracer_n, col_n), F32), pltpu.SemaphoreType.DMA((chunk_n + 1,))],
+    )(*[pltpu.with_memory_space_constraint(value, pltpu.VMEM) for value in (new, got)])
     return new.reshape(fields.shape), burden[None]
 
 

time: 21 us -> 19 us (0.905)
  local copies, waits for them, and re-layouts: 1.48 us -> 0 us
  Pallas kernels: 18.7 us -> 18.2 us
    unnamed x4 -> x0, local copies, waits for them, and re-layouts: 1.48 us -> none
    pallas_call x1, Pallas kernels: 2.27 us -> 1.17 us  [local(): pl.pallas_call(functools.partial(finish, slots, group_n, tracer_n), out_s...]
    pallas_call x1, Pallas kernels: 16.4 us -> 17 us  [local(): pl.pallas_call(functools.partial(kernel, wide_n, narrow_n, slots, group_n...]
where the time goes in v2:
time: 19 us; the launch traced here: 18.8 us
  Pallas kernels  18.2 us (96%)
  between operations  0.64 us (3%)
    pallas_call x1, Pallas kernels, local(): pl.pallas_call(functools.partial(kernel, wide_n, narrow_n, slots, group_n...  17 us
    pallas_call x1, Pallas kernels, local(): pl.pallas_call(functools.partial(finish, slots, group_n, tracer_n), out_s...  1.17 us

profile of v2, /device:TPU:0, one launch (start us, length us, event | category | flops | bytes accessed | tf_op | source)
XLA Modules:
  0.0 18.8 jit_solution(7295187731743940845)
XLA Ops:
  0.6 17.0 %shard_map.77 = (bf16[24,128,128]{2,1,0:T(8,128)(2,1)S(1)}, f32[32,256]{1,0:T(8,128)S(1)}) custom-call(bf16[24,128,128]{2,1,0:T(8,128)(2,1)} %bitcast.7, s32[4,128]{1,0:T(4,128)} %bitcast.9, s32[1,128]{1,0:T(1,128)} %cost_hbm.1, s32[1,128]{1,0:T(1,128)} %dest_hbm.1, bf16[128,128]{1,0:T(8,128)(2,1)} %bitcast.8, bf16[8,128,128]{2,1,0:T(8,128)(2,1)} %op_hbm.1), custom_call_target="tpu_custom_call" | custom-call | tf_op jit(solution)/shard_map/pallas_call | solution.py:327
  17.6 1.2 %shard_map.78 = (bf16[24,128,128]{2,1,0:T(8,128)(2,1)}, f32[24,128]{1,0:T(8,128)}) custom-call(bf16[24,128,128]{2,1,0:T(8,128)(2,1)S(1)} %get-tuple-element.6.new_ref, f32[32,256]{1,0:T(8,128)S(1)} %get-tuple-element.7.got_ref), custom_call_target="tpu_custom_call" | custom-call | tf_op jit(solution)/shard_map/pallas_call | solution.py:367

commit v3 on v2

--- a/solution.py
+++ b/solution.py
@@ -9,7 +9,7 @@
 
 REACH = 2
 EDGES = 2 * REACH
-LAG = 2
+BAND = 16
 MESH = pl.DeviceIdType.MESH
 F32 = jnp.float32
 BF16 = jnp.bfloat16
@@ -149,8 +149,10 @@
         - 2.0 * ones_at(cols == rows)
     ).astype(BF16)
     for s in range(substep_n):
-        both_ref[s, :level_n, :] = op_ref[s]
-        both_ref[s, level_n:, :] = dot(second, op_ref[s]).astype(BF16)
+        curved = dot(second, op_ref[s]).astype(BF16)
+        for begin in range(0, level_n, BAND):
+            both_ref[s, 2 * begin : 2 * begin + BAND, :] = op_ref[s, begin : begin + BAND, :]
+            both_ref[s, 2 * begin + BAND : 2 * begin + 2 * BAND, :] = curved[begin : begin + BAND]
     cost = cost_ref[...]
     gain = cost.astype(F32) / (4.0 * substep_n)
     ge = diff_ref[...].astype(F32) * gain
@@ -171,27 +173,25 @@
 
     cost_two = jnp.concatenate([cost, cost], axis=1)
 
-    def advance(s, pairs):
+    def advance(both, ref, weight_ref, live):
+        mixed = dot(both, ref[...].astype(BF16))
+        for begin in range(0, level_n, BAND):
+            band = slice(begin, begin + BAND)
+            moved = mixed[2 * begin : 2 * begin + BAND] + weight_ref[band] * mixed[2 * begin + BAND : 2 * begin + 2 * BAND]
+            ref[band] = jnp.where(live, moved, ref[band])
+
+    def advance_pairs(s, pairs):
         both = both_ref[s]
         live = cost_two > s
         for p in pairs:
-            now = cur_ref[p]
-            mixed = dot(both, now.astype(BF16))
-            moved = mixed[:level_n] + ge_ref[...] * mixed[level_n:]
-            cur_ref[p] = jnp.where(live, moved, now)
-
-    def advance_edge(s, now):
-        mixed = dot(both_ref[s], now.astype(BF16))
-        moved = mixed[:level_n] + edge_ge[...] * mixed[level_n:]
-        return jnp.where(edge_cost > jnp.asarray(s, F32), moved, now)
-
-    lag = min(LAG, substep_n)
-
-    def leading(s, carry):
-        advance(s, range(pair_n))
+            advance(both, cur_ref.at[p], ge_ref, live)
+        return both
+
+    def leading_half(s, carry):
+        advance_pairs(s, range(pair_n // 2))
         return carry
 
-    lax.fori_loop(0, lag, leading, 0)
+    lax.fori_loop(0, substep_n, leading_half, 0, unroll=2)
 
     for copy in copies:
         copy.wait()
@@ -200,16 +200,13 @@
     edge_dyn[...] = start
     edge_cur[...] = start.astype(F32)
 
-    def together(s, carry):
-        advance(s, range(pair_n))
-        edge_cur[...] = advance_edge(s - lag, edge_cur[...])
+    def other_half(s, carry):
+        both = advance_pairs(s, range(pair_n // 2, pair_n))
+        advance(both, edge_cur, edge_ge, edge_cost > jnp.asarray(s, F32))
         return carry
 
-    lax.fori_loop(lag, substep_n, together, 0)
-
+    lax.fori_loop(0, substep_n, other_half, 0, unroll=2)
     edge_end = edge_cur[...]
-    for s in range(substep_n - lag, substep_n):
-        edge_end = advance_edge(s, edge_end)
 
     col = iota((1, col_n), 1)
     inner = (col >= REACH) & (col < col_n - REACH)
@@ -311,7 +308,7 @@
     dev_n = wide_n * narrow_n
     group_n = 1 << tracer_n.bit_length()
     slots = 2 * col_n // dev_n
-    assert row_n == 1 and tracer_n % 4 == 0 and tracer_n * EDGES <= col_n and group_n <= col_n
+    assert row_n == 1 and tracer_n % 4 == 0 and level_n % BAND == 0 and tracer_n * EDGES <= col_n and group_n <= col_n
     width = -(-slots * group_n // col_n) * col_n
     hbm = pl.BlockSpec(memory_space=pltpu.HBM)
     vmem = pl.BlockSpec(memory_space=pltpu.VMEM)

time: 19 us -> 18.4 us (0.968)
  Pallas kernels: 18.2 us -> 17.6 us
    pallas_call x1, Pallas kernels: 17 us -> 16.4 us  [local(): pl.pallas_call(functools.partial(kernel, wide_n, narrow_n, slots, group_n...]
where the time goes in v3:
time: 18.4 us; the launch traced here: 18.2 us
  Pallas kernels  17.6 us (96%)
  between operations  0.64 us (3%)
    pallas_call x1, Pallas kernels, local(): pl.pallas_call(functools.partial(kernel, wide_n, narrow_n, slots, group_n...  16.4 us
    pallas_call x1, Pallas kernels, local(): pl.pallas_call(functools.partial(finish, slots, group_n, tracer_n), out_s...  1.17 us

profile of v3, /device:TPU:0, one launch (start us, length us, event | category | flops | bytes accessed | tf_op | source)
XLA Modules:
  0.0 18.2 jit_solution(12767226577651905782)
XLA Ops:
  0.6 16.4 %shard_map.77 = (bf16[24,128,128]{2,1,0:T(8,128)(2,1)S(1)}, f32[32,256]{1,0:T(8,128)S(1)}) custom-call(bf16[24,128,128]{2,1,0:T(8,128)(2,1)} %bitcast.7, s32[4,128]{1,0:T(4,128)} %bitcast.9, s32[1,128]{1,0:T(1,128)} %cost_hbm.1, s32[1,128]{1,0:T(1,128)} %dest_hbm.1, bf16[128,128]{1,0:T(8,128)(2,1)} %bitcast.8, bf16[8,128,128]{2,1,0:T(8,128)(2,1)} %op_hbm.1), custom_call_target="tpu_custom_call" | custom-call | tf_op jit(solution)/shard_map/pallas_call | solution.py:324
  17.1 1.2 %shard_map.78 = (bf16[24,128,128]{2,1,0:T(8,128)(2,1)}, f32[24,128]{1,0:T(8,128)}) custom-call(bf16[24,128,128]{2,1,0:T(8,128)(2,1)S(1)} %get-tuple-element.6.new_ref, f32[32,256]{1,0:T(8,128)S(1)} %get-tuple-element.7.got_ref), custom_call_target="tpu_custom_call" | custom-call | tf_op jit(solution)/shard_map/pallas_call | solution.py:364

commit v4 on v3

--- a/solution.py
+++ b/solution.py
@@ -92,8 +92,8 @@
     lane_q = lax.shift_right_logical(lane, shift)
     row_q = lax.shift_right_logical(src, shift)
     same_q = row_q == lane_q
-    left_of = jnp.where(row_k < REACH, lax.rem(base + row_span - REACH + row_k, row_span), -1)
-    right_of = jnp.where(row_k >= REACH, lax.rem(base + col_n + row_k - REACH, row_span), -1)
+    left_of = jnp.where(row_k < REACH, wrap(base + row_span - REACH + row_k, row_span), -1)
+    right_of = jnp.where(row_k >= REACH, wrap(base + col_n + row_k - REACH, row_span), -1)
 
     loads[0].wait()
     near = ones_at(src == lane)
@@ -187,11 +187,14 @@
             advance(both, cur_ref.at[p], ge_ref, live)
         return both
 
-    def leading_half(s, carry):
+    inner_sums = []
+
+    def add_up(q):
+        change = cur_ref[q // 2, :, (q % 2) * col_n : (q % 2 + 1) * col_n] - dyn_ref[q].astype(F32)
+        inner_sums.append(jnp.sum(change, axis=0, keepdims=True))
+
+    for s in range(substep_n):
         advance_pairs(s, range(pair_n // 2))
-        return carry
-
-    lax.fori_loop(0, substep_n, leading_half, 0, unroll=2)
 
     for copy in copies:
         copy.wait()
@@ -200,20 +203,17 @@
     edge_dyn[...] = start
     edge_cur[...] = start.astype(F32)
 
-    def other_half(s, carry):
+    for s in range(substep_n):
         both = advance_pairs(s, range(pair_n // 2, pair_n))
-        advance(both, edge_cur, edge_ge, edge_cost > jnp.asarray(s, F32))
-        return carry
-
-    lax.fori_loop(0, substep_n, other_half, 0, unroll=2)
+        advance(both, edge_cur, edge_ge, edge_cost > float(s))
+        for q in range(s * pair_n // substep_n, (s + 1) * pair_n // substep_n):
+            add_up(q)
+    for q in range(pair_n, tracer_n):
+        add_up(q)
     edge_end = edge_cur[...]
 
     col = iota((1, col_n), 1)
     inner = (col >= REACH) & (col < col_n - REACH)
-    inner_sums = []
-    for q in range(tracer_n):
-        change = cur_ref[q // 2, :, (q % 2) * col_n : (q % 2 + 1) * col_n] - dyn_ref[q].astype(F32)
-        inner_sums.append(jnp.sum(change, axis=0, keepdims=True))
     edge_start = edge_dyn[...].astype(F32)
     edge_change = edge_end - edge_start
     edge_burden = jnp.broadcast_to(jnp.sum(edge_change, axis=0, keepdims=True), (8, col_n))

time: 18.4 us -> 17.2 us (0.935)
  Pallas kernels: 17.6 us -> 16.4 us
    pallas_call x1, Pallas kernels: 16.4 us -> 15.2 us  [local(): pl.pallas_call(functools.partial(kernel, wide_n, narrow_n, slots, group_n...]
where the time goes in v4:
time: 17.2 us; the launch traced here: 17 us
  Pallas kernels  16.4 us (95%)
  between operations  0.64 us (4%)
    pallas_call x1, Pallas kernels, local(): pl.pallas_call(functools.partial(kernel, wide_n, narrow_n, slots, group_n...  15.2 us
    pallas_call x1, Pallas kernels, local(): pl.pallas_call(functools.partial(finish, slots, group_n, tracer_n), out_s...  1.17 us

profile of v4, /device:TPU:0, one launch (start us, length us, event | category | flops | bytes accessed | tf_op | source)
XLA Modules:
  0.0 17.0 jit_solution(1159102547388585754)
XLA Ops:
  0.6 15.2 %shard_map.77 = (bf16[24,128,128]{2,1,0:T(8,128)(2,1)S(1)}, f32[32,256]{1,0:T(8,128)S(1)}) custom-call(bf16[24,128,128]{2,1,0:T(8,128)(2,1)} %bitcast.7, s32[4,128]{1,0:T(4,128)} %bitcast.9, s32[1,128]{1,0:T(1,128)} %cost_hbm.1, s32[1,128]{1,0:T(1,128)} %dest_hbm.1, bf16[128,128]{1,0:T(8,128)(2,1)} %bitcast.8, bf16[8,128,128]{2,1,0:T(8,128)(2,1)} %op_hbm.1), custom_call_target="tpu_custom_call" | custom-call | tf_op jit(solution)/shard_map/pallas_call | solution.py:324
  15.9 1.2 %shard_map.78 = (bf16[24,128,128]{2,1,0:T(8,128)(2,1)}, f32[24,128]{1,0:T(8,128)}) custom-call(bf16[24,128,128]{2,1,0:T(8,128)(2,1)S(1)} %get-tuple-element.6.new_ref, f32[32,256]{1,0:T(8,128)S(1)} %get-tuple-element.7.got_ref), custom_call_target="tpu_custom_call" | custom-call | tf_op jit(solution)/shard_map/pallas_call | solution.py:364

commit v5 on v4

--- a/solution.py
+++ b/solution.py
@@ -70,7 +70,7 @@
     for index in range(chunk_n):
         part = pl.ds(index * chunk, chunk)
         x_loads.append(pltpu.make_async_copy(x_hbm.at[part], x_ref.at[part], x_sem.at[index]))
-    for load in loads[:1] + x_loads + loads[1:]:
+    for load in loads[:1] + loads[-1:] + x_loads + loads[1:-1]:
         load.start()
 
     partners = []
@@ -108,36 +108,6 @@
 
     def edge_shift(q):
         return (EDGES * q + REACH) % col_n
-
-    packed = jnp.zeros((level_n, col_n), F32)
-    partial = jnp.zeros((level_n, col_n), F32)
-    for q in range(tracer_n):
-        if q % chunk == 0:
-            x_loads[q // chunk].wait()
-        x = x_ref[q]
-        total = dot(x, near)
-        packed = jnp.where(lane_q == q, pltpu.roll(x.astype(F32), edge_shift(q), 1), packed)
-        partial = jnp.where(lane_q == q, pltpu.roll(total, edge_shift(q), 1), partial)
-        dyn = (0.2 * total).astype(BF16)
-        dyn_ref[q] = dyn
-        cur_ref[q // 2, :, (q % 2) * col_n : (q % 2 + 1) * col_n] = dyn.astype(F32)
-    pack_ref[...] = packed.astype(BF16)
-
-    pl.semaphore_wait(barrier, dev_n - 1)
-    copies = []
-    for side, step in ((0, 1), (1, narrow_n - 1)):
-        copies.append(
-            pltpu.make_async_remote_copy(
-                src_ref=pack_ref,
-                dst_ref=halo_ref.at[side],
-                send_sem=halo_send.at[side],
-                recv_sem=halo_recv.at[side],
-                device_id=(wide, wrap(narrow + step, narrow_n)),
-                device_id_type=MESH,
-            )
-        )
-    for copy in copies:
-        copy.start()
 
     for load in loads[1:]:
         load.wait()
@@ -161,7 +131,6 @@
 
     edge_cost = dot(jnp.broadcast_to(cost.astype(F32), (16, col_n)).astype(BF16), pick)[:1]
     edge_ge[...] = dot(diff_ref[...], pick) * (edge_cost / (4.0 * substep_n))
-    edge_sum[...] = partial
     edge_left = jnp.where(same_q, dot(from_left.astype(BF16), pick), 0.0).astype(BF16)
     edge_right = jnp.where(same_q, dot(from_right.astype(BF16), pick), 0.0).astype(BF16)
 
@@ -171,26 +140,53 @@
     placed = jnp.sum(hot * earlier, axis=0, keepdims=True).astype(I32)
     spot_ref[...] = ones_at(iota((slots * dev_n, col_n), 0) == placed * dev_n + dest).astype(BF16)
 
-    cost_two = jnp.concatenate([cost, cost], axis=1)
-
-    def advance(both, ref, weight_ref, live):
-        mixed = dot(both, ref[...].astype(BF16))
+    packed = jnp.zeros((level_n, col_n), F32)
+    partial = jnp.zeros((level_n, col_n), F32)
+    for q in range(tracer_n):
+        if q % chunk == 0:
+            x_loads[q // chunk].wait()
+        x = x_ref[q]
+        total = dot(x, near)
+        packed = jnp.where(lane_q == q, pltpu.roll(x.astype(F32), edge_shift(q), 1), packed)
+        partial = jnp.where(lane_q == q, pltpu.roll(total, edge_shift(q), 1), partial)
+        dyn_ref[q // 2, :, (q % 2) * col_n : (q % 2 + 1) * col_n] = (0.2 * total).astype(BF16)
+    pack_ref[...] = packed.astype(BF16)
+    edge_sum[...] = partial
+
+    pl.semaphore_wait(barrier, dev_n - 1)
+    copies = []
+    for side, step in ((0, 1), (1, narrow_n - 1)):
+        copies.append(
+            pltpu.make_async_remote_copy(
+                src_ref=pack_ref,
+                dst_ref=halo_ref.at[side],
+                send_sem=halo_send.at[side],
+                recv_sem=halo_recv.at[side],
+                device_id=(wide, wrap(narrow + step, narrow_n)),
+                device_id_type=MESH,
+            )
+        )
+    for copy in copies:
+        copy.start()
+
+    cost_two = jnp.concatenate([cost, cost], axis=1).astype(F32)
+
+    def advance(s, start_ref, ref, weight_ref, steps):
+        now = start_ref[...] if s == 0 else ref[...].astype(BF16)
+        mixed = dot(both_ref[s], now)
         for begin in range(0, level_n, BAND):
             band = slice(begin, begin + BAND)
             moved = mixed[2 * begin : 2 * begin + BAND] + weight_ref[band] * mixed[2 * begin + BAND : 2 * begin + 2 * BAND]
-            ref[band] = jnp.where(live, moved, ref[band])
+            ref[band] = moved if s == 0 else jnp.where(steps > float(s), moved, ref[band])
 
     def advance_pairs(s, pairs):
-        both = both_ref[s]
-        live = cost_two > s
         for p in pairs:
-            advance(both, cur_ref.at[p], ge_ref, live)
-        return both
+            advance(s, dyn_ref.at[p], cur_ref.at[p], ge_ref, cost_two)
 
     inner_sums = []
 
     def add_up(q):
-        change = cur_ref[q // 2, :, (q % 2) * col_n : (q % 2 + 1) * col_n] - dyn_ref[q].astype(F32)
+        change = cur_ref[q // 2, :, (q % 2) * col_n : (q % 2 + 1) * col_n] - dyn_ref[q // 2, :, (q % 2) * col_n : (q % 2 + 1) * col_n].astype(F32)
         inner_sums.append(jnp.sum(change, axis=0, keepdims=True))
 
     for s in range(substep_n):
@@ -201,11 +197,10 @@
     total = edge_sum[...] + dot(halo_ref[0], edge_left) + dot(halo_ref[1], edge_right)
     start = (0.2 * total).astype(BF16)
     edge_dyn[...] = start
-    edge_cur[...] = start.astype(F32)
 
     for s in range(substep_n):
-        both = advance_pairs(s, range(pair_n // 2, pair_n))
-        advance(both, edge_cur, edge_ge, edge_cost > float(s))
+        advance(s, edge_dyn, edge_cur, edge_ge, edge_cost)
+        advance_pairs(s, range(pair_n // 2, pair_n))
         for q in range(s * pair_n // substep_n, (s + 1) * pair_n // substep_n):
             add_up(q)
     for q in range(pair_n, tracer_n):
@@ -250,7 +245,7 @@
 
     edge_new = edge_start + edge_change.astype(BF16).astype(F32)
     for q in range(tracer_n):
-        dyn = dyn_ref[q].astype(F32)
+        dyn = dyn_ref[q // 2, :, (q % 2) * col_n : (q % 2 + 1) * col_n].astype(F32)
         change = cur_ref[q // 2, :, (q % 2) * col_n : (q % 2 + 1) * col_n] - dyn
         new = dyn + change.astype(BF16).astype(F32)
         outer = pltpu.roll(edge_new, col_n - edge_shift(q), 1)
@@ -337,7 +332,7 @@
             pltpu.VMEM((level_n, col_n), BF16),
             pltpu.VMEM((substep_n, level_n, level_n), BF16),
             pltpu.VMEM((substep_n, 2 * level_n, level_n), BF16),
-            pltpu.VMEM((tracer_n, level_n, col_n), BF16),
+            pltpu.VMEM((tracer_n // 2, level_n, 2 * col_n), BF16),
             pltpu.VMEM((tracer_n // 2, level_n, 2 * col_n), F32),
             pltpu.VMEM((level_n, 2 * col_n), F32),
             pltpu.VMEM((level_n, col_n), BF16),

time: 17.2 us -> 17.7 us (1.029)
  Pallas kernels: 16.4 us -> 16.9 us
    pallas_call x1, Pallas kernels: 15.2 us -> 15.7 us  [local(): pl.pallas_call(functools.partial(kernel, wide_n, narrow_n, slots, group_n...]
where the time goes in v5:
time: 17.7 us; the launch traced here: 17.5 us
  Pallas kernels  16.9 us (95%)
  between operations  0.64 us (4%)
    pallas_call x1, Pallas kernels, local(): pl.pallas_call(functools.partial(kernel, wide_n, narrow_n, slots, group_n...  15.7 us
    pallas_call x1, Pallas kernels, local(): pl.pallas_call(functools.partial(finish, slots, group_n, tracer_n), out_s...  1.17 us

profile of v5, /device:TPU:0, one launch (start us, length us, event | category | flops | bytes accessed | tf_op | source)
XLA Modules:
  0.0 17.5 jit_solution(12834252175809839551)
XLA Ops:
  0.6 15.7 %shard_map.77 = (bf16[24,128,128]{2,1,0:T(8,128)(2,1)S(1)}, f32[32,256]{1,0:T(8,128)S(1)}) custom-call(bf16[24,128,128]{2,1,0:T(8,128)(2,1)} %bitcast.7, s32[4,128]{1,0:T(4,128)} %bitcast.9, s32[1,128]{1,0:T(1,128)} %cost_hbm.1, s32[1,128]{1,0:T(1,128)} %dest_hbm.1, bf16[128,128]{1,0:T(8,128)(2,1)} %bitcast.8, bf16[8,128,128]{2,1,0:T(8,128)(2,1)} %op_hbm.1), custom_call_target="tpu_custom_call" | custom-call | tf_op jit(solution)/shard_map/pallas_call | solution.py:319
  16.4 1.2 %shard_map.78 = (bf16[24,128,128]{2,1,0:T(8,128)(2,1)}, f32[24,128]{1,0:T(8,128)}) custom-call(bf16[24,128,128]{2,1,0:T(8,128)(2,1)S(1)} %get-tuple-element.6.new_ref, f32[32,256]{1,0:T(8,128)S(1)} %get-tuple-element.7.got_ref), custom_call_target="tpu_custom_call" | custom-call | tf_op jit(solution)/shard_map/pallas_call | solution.py:359

commit v6 on v4

--- a/solution.py
+++ b/solution.py
@@ -45,7 +45,7 @@
     x_hbm, nb_hbm, cost_hbm, dest_hbm, diff_hbm, op_hbm,
     new_ref, got_ref,
     x_ref, nb_ref, cost_ref, dest_ref, diff_ref, op_ref,
-    both_ref, dyn_ref, cur_ref, ge_ref, pack_ref, halo_ref,
+    both_ref, dyn_ref, cur_ref, first_sum, end_sum, edge_tot, ge_ref, pack_ref, halo_ref,
     edge_ge, edge_sum, edge_dyn, edge_cur, spot_ref, sums_ref, out_slots, in_slots,
     in_sem, x_sem, halo_send, halo_recv, slot_send, slot_recv,
 ):
@@ -119,9 +119,11 @@
         packed = jnp.where(lane_q == q, pltpu.roll(x.astype(F32), edge_shift(q), 1), packed)
         partial = jnp.where(lane_q == q, pltpu.roll(total, edge_shift(q), 1), partial)
         dyn = (0.2 * total).astype(BF16)
-        dyn_ref[q] = dyn
-        cur_ref[q // 2, :, (q % 2) * col_n : (q % 2 + 1) * col_n] = dyn.astype(F32)
+        half = slice((q % 2) * col_n, (q % 2 + 1) * col_n)
+        dyn_ref[q // 2, :, half] = dyn
+        first_sum[q // 2, :, half] = jnp.sum(dyn.astype(F32), axis=0, keepdims=True)
     pack_ref[...] = packed.astype(BF16)
+    edge_sum[...] = partial
 
     pl.semaphore_wait(barrier, dev_n - 1)
     copies = []
@@ -161,7 +163,6 @@
 
     edge_cost = dot(jnp.broadcast_to(cost.astype(F32), (16, col_n)).astype(BF16), pick)[:1]
     edge_ge[...] = dot(diff_ref[...], pick) * (edge_cost / (4.0 * substep_n))
-    edge_sum[...] = partial
     edge_left = jnp.where(same_q, dot(from_left.astype(BF16), pick), 0.0).astype(BF16)
     edge_right = jnp.where(same_q, dot(from_right.astype(BF16), pick), 0.0).astype(BF16)
 
@@ -171,27 +172,25 @@
     placed = jnp.sum(hot * earlier, axis=0, keepdims=True).astype(I32)
     spot_ref[...] = ones_at(iota((slots * dev_n, col_n), 0) == placed * dev_n + dest).astype(BF16)
 
-    cost_two = jnp.concatenate([cost, cost], axis=1)
-
-    def advance(both, ref, weight_ref, live):
-        mixed = dot(both, ref[...].astype(BF16))
+    cost_two = jnp.concatenate([cost, cost], axis=1).astype(F32)
+
+    def advance(s, start_ref, ref, sum_ref, weight_ref, steps):
+        now = start_ref[...] if s == 0 else ref[...]
+        mixed = dot(both_ref[s], now)
+        live = jnp.broadcast_to(steps.astype(BF16), (BAND, steps.shape[1])) > jnp.asarray(s, BF16)
+        added = jnp.zeros((BAND, steps.shape[1]), F32)
         for begin in range(0, level_n, BAND):
             band = slice(begin, begin + BAND)
             moved = mixed[2 * begin : 2 * begin + BAND] + weight_ref[band] * mixed[2 * begin + BAND : 2 * begin + 2 * BAND]
-            ref[band] = jnp.where(live, moved, ref[band])
+            added += moved
+            rounded = moved.astype(BF16)
+            ref[band] = rounded if s == 0 else jnp.where(live, rounded, now[band])
+        added = jnp.sum(added, axis=0, keepdims=True)
+        sum_ref[...] = added if s == 0 else jnp.where(steps > float(s), added, sum_ref[...])
 
     def advance_pairs(s, pairs):
-        both = both_ref[s]
-        live = cost_two > s
         for p in pairs:
-            advance(both, cur_ref.at[p], ge_ref, live)
-        return both
-
-    inner_sums = []
-
-    def add_up(q):
-        change = cur_ref[q // 2, :, (q % 2) * col_n : (q % 2 + 1) * col_n] - dyn_ref[q].astype(F32)
-        inner_sums.append(jnp.sum(change, axis=0, keepdims=True))
+            advance(s, dyn_ref.at[p], cur_ref.at[p], end_sum.at[p], ge_ref, cost_two)
 
     for s in range(substep_n):
         advance_pairs(s, range(pair_n // 2))
@@ -201,26 +200,24 @@
     total = edge_sum[...] + dot(halo_ref[0], edge_left) + dot(halo_ref[1], edge_right)
     start = (0.2 * total).astype(BF16)
     edge_dyn[...] = start
-    edge_cur[...] = start.astype(F32)
 
     for s in range(substep_n):
-        both = advance_pairs(s, range(pair_n // 2, pair_n))
-        advance(both, edge_cur, edge_ge, edge_cost > float(s))
-        for q in range(s * pair_n // substep_n, (s + 1) * pair_n // substep_n):
-            add_up(q)
-    for q in range(pair_n, tracer_n):
-        add_up(q)
-    edge_end = edge_cur[...]
+        advance(s, edge_dyn, edge_cur, edge_tot, edge_ge, edge_cost)
+        advance_pairs(s, range(pair_n // 2, pair_n))
 
     col = iota((1, col_n), 1)
     inner = (col >= REACH) & (col < col_n - REACH)
     edge_start = edge_dyn[...].astype(F32)
-    edge_change = edge_end - edge_start
-    edge_burden = jnp.broadcast_to(jnp.sum(edge_change, axis=0, keepdims=True), (8, col_n))
+    edge_change = edge_cur[...].astype(F32) - edge_start
+    edge_burden = jnp.broadcast_to(
+        edge_tot[...] - jnp.sum(edge_start, axis=0, keepdims=True), (8, col_n)
+    )
     sums_ref[...] = jnp.ones(sums_ref.shape, F32)
     for q in range(tracer_n):
         outer = pltpu.roll(edge_burden, col_n - edge_shift(q), 1)[:1]
-        sums_ref[q : q + 1, :] = jnp.where(inner, inner_sums[q], outer)
+        half = slice((q % 2) * col_n, (q % 2 + 1) * col_n)
+        own = end_sum[q // 2, :, half] - first_sum[q // 2, :, half]
+        sums_ref[q : q + 1, :] = jnp.where(inner, own, outer)
     per_row = col_n // group_n
     sums = sums_ref[...]
     sums = jnp.concatenate([sums] * per_row, axis=0)
@@ -250,8 +247,8 @@
 
     edge_new = edge_start + edge_change.astype(BF16).astype(F32)
     for q in range(tracer_n):
-        dyn = dyn_ref[q].astype(F32)
-        change = cur_ref[q // 2, :, (q % 2) * col_n : (q % 2 + 1) * col_n] - dyn
+        dyn = dyn_ref[q // 2, :, (q % 2) * col_n : (q % 2 + 1) * col_n].astype(F32)
+        change = cur_ref[q // 2, :, (q % 2) * col_n : (q % 2 + 1) * col_n].astype(F32) - dyn
         new = dyn + change.astype(BF16).astype(F32)
         outer = pltpu.roll(edge_new, col_n - edge_shift(q), 1)
         new_ref[q] = jnp.where(inner, new, outer).astype(BF16)
@@ -337,15 +334,18 @@
             pltpu.VMEM((level_n, col_n), BF16),
             pltpu.VMEM((substep_n, level_n, level_n), BF16),
             pltpu.VMEM((substep_n, 2 * level_n, level_n), BF16),
-            pltpu.VMEM((tracer_n, level_n, col_n), BF16),
-            pltpu.VMEM((tracer_n // 2, level_n, 2 * col_n), F32),
+            pltpu.VMEM((tracer_n // 2, level_n, 2 * col_n), BF16),
+            pltpu.VMEM((tracer_n // 2, level_n, 2 * col_n), BF16),
+            pltpu.VMEM((tracer_n // 2, 1, 2 * col_n), F32),
+            pltpu.VMEM((tracer_n // 2, 1, 2 * col_n), F32),
+            pltpu.VMEM((1, col_n), F32),
             pltpu.VMEM((level_n, 2 * col_n), F32),
             pltpu.VMEM((level_n, col_n), BF16),
             pltpu.VMEM((2, level_n, col_n), BF16),
             pltpu.VMEM((level_n, col_n), F32),
             pltpu.VMEM((level_n, col_n), F32),
             pltpu.VMEM((level_n, col_n), BF16),
-            pltpu.VMEM((level_n, col_n), F32),
+            pltpu.VMEM((level_n, col_n), BF16),
             pltpu.VMEM((slots * dev_n, col_n), BF16),
             pltpu.VMEM((group_n, col_n), F32),
             pltpu.VMEM((dev_n, 1, width), F32),

time: 17.2 us -> 17.3 us (level)
  no operation moved by 1% of the time
where the time goes in v6:
time: 17.3 us; the launch traced here: 17.1 us
  Pallas kernels  16.5 us (95%)
  between operations  0.64 us (4%)
    pallas_call x1, Pallas kernels, local(): pl.pallas_call(functools.partial(kernel, wide_n, narrow_n, slots, group_n...  15.3 us
    pallas_call x1, Pallas kernels, local(): pl.pallas_call(functools.partial(finish, slots, group_n, tracer_n), out_s...  1.17 us

profile of v6, /device:TPU:0, one launch (start us, length us, event | category | flops | bytes accessed | tf_op | source)
XLA Modules:
  0.0 17.1 jit_solution(14650129079787952206)
XLA Ops:
  0.6 15.3 %shard_map.77 = (bf16[24,128,128]{2,1,0:T(8,128)(2,1)S(1)}, f32[32,256]{1,0:T(8,128)S(1)}) custom-call(bf16[24,128,128]{2,1,0:T(8,128)(2,1)} %bitcast.7, s32[4,128]{1,0:T(4,128)} %bitcast.9, s32[1,128]{1,0:T(1,128)} %cost_hbm.1, s32[1,128]{1,0:T(1,128)} %dest_hbm.1, bf16[128,128]{1,0:T(8,128)(2,1)} %bitcast.8, bf16[8,128,128]{2,1,0:T(8,128)(2,1)} %op_hbm.1), custom_call_target="tpu_custom_call" | custom-call | tf_op jit(solution)/shard_map/pallas_call | solution.py:321
  15.9 1.2 %shard_map.78 = (bf16[24,128,128]{2,1,0:T(8,128)(2,1)}, f32[24,128]{1,0:T(8,128)}) custom-call(bf16[24,128,128]{2,1,0:T(8,128)(2,1)S(1)} %get-tuple-element.6.new_ref, f32[32,256]{1,0:T(8,128)S(1)} %get-tuple-element.7.got_ref), custom_call_target="tpu_custom_call" | custom-call | tf_op jit(solution)/shard_map/pallas_call | solution.py:364
